TPU v7x, 32 devices: a whole 2x2x4 slice. The times are simulated.
32 devices in a mesh: pair: 8 (over y, x, core), cores: 4 (over z).
Axes of the slice: x: 2, y: 2, z: 4, core: 2. Of those that a mesh axis runs over, the one named last changes fastest.
Arguments:
- basis_rows: bfloat16 [16384, 2048], P('pair'), may hold values from -0.046875 to 0.046875
- energies: float32 [16384], P('pair'), may hold values from 0.5 to 4
- integrals: bfloat16 [16384, 4096], P('pair', 'cores'), may hold values from -0.75 to 0.75
- core_amps: bfloat16 [2048, 2048], P(('pair', 'cores')), may hold values from -3 to 3
- denominators: float32 [2048], replicated, may hold values from 1 to 4
Outputs:
- core_next: float32 [2048, 2048], P(('pair', 'cores'))
- amplitudes: bfloat16 [16384, 2048], P('pair')
All inputs are finite; a program needn't handle non-finite values.
Results may differ from a plain program's by a relative error of at most 0.0056.
Values may be sent and summed in bfloat16 or wider, within the bound.
A program may use at most 128 MiB of HBM per device.

v0:
```python
import jax
import jax.numpy as jnp
from jax import lax
from jax.sharding import PartitionSpec as P


def contract_rows(left, right):
    return lax.dot_general(
        left, right, (((0,), (0,)), ((), ())), preferred_element_type=jnp.float32
    )


def local(basis_rows, energies, integrals, core_amps, denominators):
    pair_count = lax.axis_size("pair")
    core_count = lax.axis_size("cores")
    slab_rows, core_order = basis_rows.shape
    core_block = core_amps.shape[0]
    core_index = lax.axis_index("cores")
    owner_index = lax.axis_index("pair") * core_count + core_index
    partial_value = contract_rows(basis_rows, integrals)
    projected = lax.psum_scatter(partial_value, "pair", scatter_dimension=0, tiled=True)
    projected_b = projected.astype(jnp.bfloat16)
    proj_all = lax.all_gather(projected_b, "pair", axis=0, tiled=True)
    weighted = (energies[:, None] * basis_rows.astype(jnp.float32)).astype(jnp.bfloat16)
    grouped = basis_rows.reshape(slab_rows, pair_count, core_count, core_block)
    basis_keep = lax.dynamic_index_in_dim(grouped, core_index, 2, keepdims=False)
    basis_keep = basis_keep.reshape(slab_rows, pair_count * core_block)
    columns = weighted
    fock_rows_f = lax.psum_scatter(
        contract_rows(columns, basis_keep), "pair", scatter_dimension=0, tiled=True
    )
    fock_rows_b = fock_rows_f.astype(jnp.bfloat16)
    matching = lax.all_gather(core_amps, "pair", axis=0, tiled=True)
    term = lax.dot_general(
        projected_b, proj_all, (((1,), (1,)), ((), ())), preferred_element_type=jnp.float32
    )
    term = term + jnp.dot(fock_rows_b, matching, preferred_element_type=jnp.float32)
    coulomb = lax.psum_scatter(term, "cores", scatter_dimension=0, tiled=True)
    own_denoms = lax.dynamic_slice_in_dim(denominators, owner_index * core_block, core_block, 0)
    core_next = core_amps.astype(jnp.float32) - coulomb / (
        own_denoms[:, None] + denominators[None, :]
    )
    core_b = core_next.astype(jnp.bfloat16)
    columns = basis_rows
    summed = jnp.dot(
        columns,
        lax.all_gather(core_b, ("pair", "cores"), axis=0, tiled=True),
        preferred_element_type=jnp.float32,
    )
    amplitudes = summed.astype(jnp.bfloat16)
    return (core_next, amplitudes)


def solution(mesh):
    in_specs = (P("pair", None), P("pair"), P("pair", "cores"), P(("pair", "cores"), None), P())
    out_specs = (P(("pair", "cores"), None), P("pair", None))
    return jax.shard_map(local, mesh=mesh, in_specs=in_specs, out_specs=out_specs, check_vma=False)
```

profile of v0, /device:TPU:26, one launch (start us, length us, event | category | flops | bytes accessed | tf_op | source)
XLA Modules:
  0.0 388.9 jit_solution(7531207068110742928)
XLA Ops:
  7.2 0.0 reduce-scatter.4.cloned.1.call-start
  7.2 14.6 %fusion.4 = f32[2048,1024]{1,0:T(8,128)} fusion(bf16[2048,2048]{1,0:T(8,128)(2,1)} %param.5, bf16[2048,1024]{1,0:T(8,128)(2,1)} %param.7), kind=kOutput, calls=%fused_computation.9 | convolution fusion | flops 8589934592 | bytes 20971520 | tf_op jit(solution)/shard_map/dot_general | solution.py:8
  21.9 0.0 reduce-scatter.4.cloned.1.call-update
  21.9 0.0 all-gather.4.cloned.1.call-start
  21.9 72.2 %reduce-scatter.4.cloned.1.call-done = f32[256,1024]{1,0:T(8,128)} async-done(((f32[2048,1024]{1,0:T(8,128)}), f32[256,1024]{1,0:T(8,128)}) %reduce-scatter.4.cloned.1.call-update) | async-done | bytes 1048592 | tf_op jit(solution)/shard_map/reduce_scatter | solution.py:21
  94.2 2.1 convert_element_type.25
  96.2 0.0 all-gather.4.cloned.1.call-update
  96.3 0.0 all-gather.6.cloned.1.call-start
  96.3 0.7 all-gather.6.cloned.1.call-update
  97.0 0.0 reduce-scatter.6.cloned.1.call-start
  97.1 0.0 copy-start.3
  97.1 12.3 %copy.8 = bf16[2048,2048]{0,1:T(8,128)(2,1)} copy(bf16[2048,2048]{1,0:T(8,128)(2,1)} %param.5) | data formatting | bytes 16777216 | tf_op args[0]
  109.4 1.7 constant_dynamic-slice_fusion
  111.1 0.0 copy-start
  111.1 11.2 %fusion = f32[2048,512]{1,0:T(8,128)} fusion(bf16[2048,512]{0,1:T(8,128)(2,1)S(1)} %bitcast.13, bf16[2048,2048]{1,0:T(8,128)(2,1)} %param.5, f32[2048]{0:T(1024)S(1)} %copy-done.3), kind=kOutput, calls=%fused_computation.1 | convolution fusion | flops 4307550208 | bytes 14688256 | tf_op jit(solution)/shard_map/dot_general | solution.py:8
  122.3 0.0 reduce-scatter.6.cloned.1.call-update
  122.3 0.0 copy-start.2
  122.3 0.0 reduce-scatter.8.cloned.1.call-start
  122.4 11.2 %all-gather.4.cloned.1.call-done = bf16[2048,1024]{1,0:T(8,128)(2,1)} async-done(((bf16[256,1024]{1,0:T(8,128)(2,1)}), bf16[2048,1024]{1,0:T(8,128)(2,1)}) %all-gather.4.cloned.1.call-update) | async-done | bytes 4194320 | tf_op jit(solution)/shard_map/all_gather | solution.py:23
  133.6 3.5 fusion.5
  137.1 26.6 %all-gather.6.cloned.1.call-done = bf16[512,2048]{1,0:T(8,128)(2,1)} async-done(((bf16[64,2048]{1,0:T(8,128)(2,1)}), bf16[512,2048]{1,0:T(8,128)(2,1)}) %all-gather.6.cloned.1.call-update) | async-done | bytes 2097168 | tf_op jit(solution)/shard_map/all_gather | solution.py:33
  163.6 55.5 %reduce-scatter.6.cloned.1.call-done = f32[256,512]{1,0:T(8,128)} async-done(((f32[2048,512]{1,0:T(8,128)}), f32[256,512]{1,0:T(8,128)}) %reduce-scatter.6.cloned.1.call-update) | async-done | bytes 524304 | tf_op jit(solution)/shard_map/reduce_scatter | solution.py:29
  219.1 3.8 convolution_add_fusion
  222.9 0.0 reduce-scatter.8.cloned.1.call-update
  222.9 0.2 all-gather.8.cloned.1.call-start
  223.2 0.1 dynamic_slice.8
  223.3 42.1 %reduce-scatter.8.cloned.1.call-done = f32[64,2048]{1,0:T(8,128)} async-done(((f32[256,2048]{1,0:T(8,128)}), f32[64,2048]{1,0:T(8,128)}) %reduce-scatter.8.cloned.1.call-update) | async-done | bytes 524304 | tf_op jit(solution)/shard_map/reduce_scatter | solution.py:38
  265.3 2.1 fusion.3
  267.4 0.0 all-gather.8.cloned.1.call-update
  267.5 78.6 %all-gather.8.cloned.1.call-done = bf16[2048,2048]{1,0:T(8,128)(2,1)} async-done(((bf16[64,2048]{1,0:T(8,128)(2,1)}), bf16[2048,2048]{1,0:T(8,128)(2,1)}) %all-gather.8.cloned.1.call-update) | async-done | bytes 8388624 | tf_op jit(solution)/shard_map/all_gather | solution.py:47
  346.0 23.8 %convert_bitcast_fusion = bf16[2048,2048]{0,1:T(8,128)(2,1)} fusion(bf16[2048,2048]{1,0:T(8,128)(2,1)} %all-gather.8.cloned.1.call-done, bf16[2048,2048]{1,0:T(8,128)(2,1)} %param.5), kind=kOutput, calls=%fused_computation.2 | convolution fusion | flops 17184063488 | bytes 25165824 | tf_op jit(solution)/shard_map/dot_general | solution.py:45
  369.8 12.2 %copy.9 = bf16[2048,2048]{1,0:T(8,128)(2,1)} copy(bf16[2048,2048]{0,1:T(8,128)(2,1)} %convert_bitcast_fusion) | data formatting | bytes 16777216
  (5 shorter events, 0.0 us)
Async XLA Ops:
  7.2 87.0 %reduce-scatter.4.cloned.1.call-start = ((), (), s32[]{:S(2)}) async-start(), calls=%async_computation.3 | async-start | bytes 9437184 | tf_op jit(solution)/shard_map/reduce_scatter | solution.py:21
  21.9 111.7 %all-gather.4.cloned.1.call-start = ((), (), s32[]{:S(2)}) async-start(), calls=%async_computation.4 | async-start | bytes 4718592 | tf_op jit(solution)/shard_map/all_gather | solution.py:23
  96.3 67.4 %all-gather.6.cloned.1.call-start = ((), (), s32[]{:S(2)}) async-start(), calls=%async_computation.6 | async-start | bytes 2359296 | tf_op jit(solution)/shard_map/all_gather | solution.py:33
  97.0 122.1 %reduce-scatter.6.cloned.1.call-start = ((), (), s32[]{:S(2)}) async-start(), calls=%async_computation.5 | async-start | bytes 4718592 | tf_op jit(solution)/shard_map/reduce_scatter | solution.py:29
  97.1 14.0 %copy-start.3 = (f32[2048]{0:T(1024)S(1)}, f32[2048]{0:T(1024)}, u32[]{:S(2)}) copy-start(f32[2048]{0:T(1024)} %param.6) | copy-start | bytes 24580
  111.1 22.5 %copy-start = (bf16[256,1024]{1,0:T(8,128)(2,1)S(1)}, bf16[256,1024]{1,0:T(8,128)(2,1)}, u32[]{:S(2)}) copy-start(bf16[256,1024]{1,0:T(8,128)(2,1)} %convert_element_type.25) | copy-start | bytes 1572868
  122.3 100.9 %copy-start.2 = (f32[2048]{0:T(1024)S(1)}, f32[2048]{0:T(1024)}, u32[]{:S(2)}) copy-start(f32[2048]{0:T(1024)} %param.9) | copy-start | bytes 24580
  122.3 143.0 %copy-start.1 = (bf16[64,2048]{1,0:T(8,128)(2,1)S(1)}, bf16[64,2048]{1,0:T(8,128)(2,1)}, u32[]{:S(2)}) copy-start(bf16[64,2048]{1,0:T(8,128)(2,1)} %param.8) | copy-start | bytes 786436
  122.3 143.0 %reduce-scatter.8.cloned.1.call-start = ((), (), s32[]{:S(2)}) async-start(), calls=%async_computation.7 | async-start | bytes 2621440 | tf_op jit(solution)/shard_map/reduce_scatter | solution.py:38
  222.9 123.1 %all-gather.8.cloned.1.call-start = ((), (), s32[]{:S(2)}) async-start(), calls=%async_computation.8 | async-start | bytes 8650752 | tf_op jit(solution)/shard_map/all_gather | solution.py:47
Sparse Core Ops, SparseCore 0:
  22.0 72.1 reduce-scatter.3
  96.8 36.7 all-gather.3
  135.7 27.9 all-gather.5
  167.8 51.2 reduce-scatter.5
  223.1 42.2 reduce-scatter.7
  269.1 76.8 all-gather.7
where the time goes:
time: 393 us; the launch traced here: 389 us
  waiting for transfers between devices  287 us (73%)
  matrix products  56.9 us (14%)
  local copies, waits for them, and re-layouts  26.4 us (7%)
  between operations  14.2 us (4%)
  other arithmetic  4.18 us (1%)
    all_gather x1, waiting for transfers between devices, local(): lax.all_gather(core_b, ('pair', 'cores'), axis=0, tiled=True)  78.6 us
    reduce_scatter x1, waiting for transfers between devices, local(): lax.psum_scatter(partial_value, 'pair', scatter_dimension=0, tiled=True)  72.2 us
    reduce_scatter x1, waiting for transfers between devices, local(): lax.psum_scatter(contract_rows(columns, basis_keep), 'pair', scatter_dime...  55.5 us
    reduce_scatter x1, waiting for transfers between devices, local(): coulomb = lax.psum_scatter(term, 'cores', scatter_dimension=0, tiled=True)  42.1 us
    all_gather x1, waiting for transfers between devices, local(): matching = lax.all_gather(core_amps, 'pair', axis=0, tiled=True)  26.6 us
    dot_general x2, matrix products, contract_rows(): lax.dot_general(left, right, (((0,), (0,)), ((), ())), preferred_element_...  25.8 us
    unnamed x10, local copies, waits for them, and re-layouts  24.5 us
    dot_general x1, matrix products, local(): jnp.dot(columns, lax.all_gather(core_b, ('pair', 'cores'), axis=0, tiled=...  23.8 us
  transfers between devices with their start and end apart: 6, of which 6 were waited for; matrix products, arithmetic and copies ran while one was open for 7% of the time, Pallas kernels for 0%

commit v1 on v0

v1 whole, which is shorter than its diff:
```python
import functools

import jax
import jax.numpy as jnp
from jax import lax
from jax.experimental import pallas as pl
from jax.experimental.pallas import tpu as pltpu
from jax.sharding import PartitionSpec as P

F32 = jnp.float32
BF16 = jnp.bfloat16
MESH = pl.DeviceIdType.MESH


def dot_nn(left, right):
    return lax.dot_general(left, right, (((1,), (0,)), ((), ())), preferred_element_type=F32)


def dot_nt(left, right):
    return lax.dot_general(left, right, (((1,), (1,)), ((), ())), preferred_element_type=F32)


def one_hot(rows, columns, column_of):
    row = lax.broadcasted_iota(jnp.int32, (rows, columns), 0)
    column = lax.broadcasted_iota(jnp.int32, (rows, columns), 1)
    return jnp.where(column == column_of(row), 1.0, 0.0).astype(BF16)


def kernel(
    n, m, H,
    basis_hbm, energies, integrals_hbm, core_hbm, own_denoms, denoms,
    next_ref, amps_hbm,
    basis, ints, left, sib_out, sib_in, summed, peer_in, final, final_t, p_all, c_all,
    term, term_b, z_in, core_all, stage,
    load_sem, out_sem, c_send, c_fwd, c_recv, s_send, s_recv, x_send, x_recv,
    p_send, p_fwd, p_recv, z_send, z_recv, zg_send, g_send, g_fwd, g_recv,
):
    me, z = lax.axis_index("pair"), lax.axis_index("cores")
    nc = n // 2
    chip, c = me // 2, lax.rem(me, 2)
    sib = chip * 2 + 1 - c
    S, R = basis.shape
    A = ints.shape[1]
    K, blk = R // m, R // n
    o = blk // m
    w = R // H
    D = A + K
    TM = D // 3

    def peer(i):
        return lax.rem(chip + i, nc) * 2 + c

    def back(i):
        return lax.rem(chip + nc - i, nc) * 2 + c

    def other(i):
        return lax.rem(chip + nc - i, nc) * 2 + 1 - c

    def rc(src, dst, ssem, rsem, pair, zz):
        return pltpu.make_async_remote_copy(
            src_ref=src, dst_ref=dst, send_sem=ssem, recv_sem=rsem,
            device_id=(pair, zz), device_id_type=MESH,
        )

    load_i = pltpu.make_async_copy(integrals_hbm, ints, load_sem.at[0])
    load_b = pltpu.make_async_copy(basis_hbm, basis, load_sem.at[1])

    def c_rows(s):
        return c_all.at[pl.ds(pl.multiple_of(s * o, o), o), :]

    load_c = pltpu.make_async_copy(core_hbm, c_rows(me), load_sem.at[2])
    load_c.start()
    load_i.start()
    load_b.start()

    barrier = pltpu.get_barrier_semaphore()
    pl.semaphore_signal(barrier, inc=1, device_id=(sib, z), device_id_type=MESH)
    for i in range(1, nc):
        pl.semaphore_signal(barrier, inc=1, device_id=(peer(i), z), device_id_type=MESH)
    for j in range(1, m):
        pl.semaphore_signal(
            barrier, inc=1, device_id=(me, lax.rem(z + j, m)), device_id_type=MESH
        )
    pl.semaphore_wait(barrier, nc + m - 1)

    def gather_start(slot, send, recv):
        for i in range(nc):
            to = sib if i == 0 else peer(i)
            rc(slot(me), slot(me), send.at[i], recv.at[me], to, z).start()

    def gather_forward(slot, fwd, recv):
        for i in range(1, nc):
            s = back(i)
            copy = rc(slot(s), slot(s), fwd.at[i], recv.at[s], sib, z)
            copy.wait_recv()
            copy.start()

    def gather_finish(slot, send, fwd, recv):
        for i in range(nc):
            s = other(i)
            rc(slot(s), slot(s), send.at[i], recv.at[s], sib, z).wait_recv()
        for i in range(nc):
            rc(slot(me), slot(me), send.at[i], recv.at[me], sib, z).wait_send()
            if i:
                rc(slot(me), slot(me), fwd.at[i], recv.at[me], sib, z).wait_send()

    load_c.wait()
    gather_start(c_rows, c_send, c_recv)

    load_i.wait()
    TA = 256
    eye = one_hot(TA, TA, lambda row: row)

    @pl.loop(0, A // TA)
    def _(t):
        at = pl.multiple_of(t * TA, TA)
        left[pl.ds(at, TA), :] = dot_nt(eye, ints[:, pl.ds(at, TA)]).astype(BF16)

    load_b.wait()
    TK = 128
    pick = one_hot(TK, TK * m, lambda row: (row // o) * blk + z * o + lax.rem(row, o))

    @pl.loop(0, K // TK)
    def _(t):
        kept = dot_nt(pick, basis[:, pl.ds(pl.multiple_of(t * TK * m, TK * m), TK * m)])
        left[pl.ds(pl.multiple_of(A + t * TK, TK), TK), :] = (kept * energies[...]).astype(BF16)

    def sib_copy(i):
        return rc(sib_out.at[i], sib_in.at[i], s_send.at[i], s_recv.at[i], sib, z)

    def peer_copy(i):
        return rc(summed.at[i], peer_in.at[i], x_send.at[i], x_recv.at[i], peer(i), z)

    def partial_block(pair, dst):
        col = pl.ds(pl.multiple_of(pair * blk, blk), blk)

        @pl.loop(0, 3)
        def _(t):
            rows = pl.ds(pl.multiple_of(t * TM, TM), TM)
            dst[rows, :] = dot_nn(left[rows, :], basis[:, col]).astype(BF16)

    def combine(i):
        sib_copy(i).wait_recv()

        @pl.loop(0, D // 128)
        def _(t):
            rows = pl.ds(pl.multiple_of(t * 128, 128), 128)
            summed[i, rows, :] = (
                summed[i, rows, :].astype(F32) + sib_in[i, rows, :].astype(F32)
            ).astype(BF16)

        peer_copy(i).start()

    order = list(range(nc - 1, 0, -1)) + [0]
    for k, i in enumerate(order):
        to = peer(i)
        partial_block(to + 1 - 2 * c, sib_out.at[i])
        sib_copy(i).start()
        if k >= 1:
            combine(order[k - 1])
        partial_block(to, summed.at[i])

    gather_forward(c_rows, c_fwd, c_recv)
    sib_copy(0).wait_recv()
    for i in range(1, nc):
        peer_copy(i).wait_recv()

    @pl.loop(0, D // 128)
    def _(t):
        rows = pl.ds(pl.multiple_of(t * 128, 128), 128)
        total = summed[0, rows, :].astype(F32) + sib_in[0, rows, :].astype(F32)
        for i in range(1, nc):
            total += peer_in[i, rows, :].astype(F32)
        final[rows, :] = total.astype(BF16)

    def p_slot(s):
        return p_all.at[s]

    p_all[me] = final[0:A, :]
    gather_start(p_slot, p_send, p_recv)
    final_t[...] = dot_nt(one_hot(blk, blk, lambda row: row), final[...]).astype(BF16)
    gather_finish(c_rows, c_send, c_fwd, c_recv)
    gather_forward(p_slot, p_fwd, p_recv)
    gather_finish(p_slot, p_send, p_fwd, p_recv)

    per = n // H

    def z_copy(h, j):
        zz = lax.rem(z + j, m)
        rows = pl.ds(pl.multiple_of(zz * o, o), o)
        return rc(term_b.at[h, rows, :], z_in.at[h, j], z_send.at[h, j], z_recv.at[h, j], me, zz)

    for h in range(H):
        @pl.loop(0, per)
        def _(k):
            q = h * per + k
            value = dot_nn(final_t[:, 0:A], p_all[q])
            value += dot_nn(
                final_t[:, A:D], c_all[:, pl.ds(pl.multiple_of(q * blk, blk), blk)]
            )
            col = pl.ds(pl.multiple_of(k * blk, blk), blk)
            term[h, :, col] = value
            term_b[h, :, col] = value.astype(BF16)

        for j in range(1, m):
            z_copy(h, j).start()

    own = me * m + z

    def slot(h, owner):
        return core_all.at[h, pl.ds(pl.multiple_of(owner * o, o), o), :]

    def core_copy(h, owner, ssem, pair, zz):
        return rc(slot(h, owner), slot(h, owner), ssem, g_recv.at[h, owner], pair, zz)

    def spread(h, j, owner):
        for i in range(1, nc):
            core_copy(h, owner, g_send.at[h, j, i], peer(i), z).start()
        core_copy(h, owner, g_send.at[h, j, 0], sib, z).start()

    for h in range(H):
        for j in range(1, m):
            z_copy(h, j).wait_recv()
        cols = pl.ds(h * w, w)
        total = term[h, pl.ds(pl.multiple_of(z * o, o), o), :]
        for j in range(1, m):
            total += z_in[h, j].astype(F32)
        current = c_all[pl.ds(pl.multiple_of(me * o, o), o), cols].astype(F32)
        value = current - total / (own_denoms[...] + denoms[:, cols])
        next_ref[:, cols] = value
        core_all[h, pl.ds(pl.multiple_of(own * o, o), o), :] = value.astype(BF16)
        for j in range(1, m):
            core_copy(h, own, zg_send.at[h, j], me, lax.rem(z + j, m)).start()
        spread(h, 0, own)

    for h in range(H):
        @pl.loop(1, m)
        def _(j):
            owner = me * m + lax.rem(z + m - j, m)
            core_copy(h, owner, g_send.at[h, j, 0], sib, z).wait_recv()
            spread(h, j, owner)

    TR, TN = 512, 256
    writes = []
    for h in range(H):
        @pl.loop(0, m)
        def _(j):
            for i in range(1, nc):
                owner = back(i) * m + lax.rem(z + m - j, m)
                copy = core_copy(h, owner, g_fwd.at[h, j, i], sib, z)
                copy.wait_recv()
                copy.start()

        @pl.loop(0, m)
        def _(j):
            for i in range(nc):
                owner = other(i) * m + lax.rem(z + m - j, m)
                core_copy(h, owner, g_send.at[h, j, i], sib, z).wait_recv()

        for t in range(S // TR):
            b = len(writes) % 2
            if len(writes) >= 2:
                writes[-2].wait()

            @pl.loop(0, w // TN)
            def _(k):
                col = pl.ds(pl.multiple_of(k * TN, TN), TN)
                stage[b, :, col] = dot_nn(
                    basis[t * TR:(t + 1) * TR, :], core_all[h, :, col]
                ).astype(BF16)

            copy = pltpu.make_async_copy(
                stage.at[b], amps_hbm.at[pl.ds(t * TR, TR), pl.ds(h * w, w)], out_sem.at[b]
            )
            copy.start()
            writes.append(copy)
    for copy in writes[-2:]:
        copy.wait()

    for i in range(nc):
        sib_copy(i).wait_send()
        if i:
            peer_copy(i).wait_send()
    for h in range(H):
        for j in range(1, m):
            z_copy(h, j).wait_send()
            core_copy(h, own, zg_send.at[h, j], sib, z).wait_send()

        @pl.loop(0, m)
        def _(j):
            for i in range(nc):
                core_copy(h, own, g_send.at[h, j, i], sib, z).wait_send()
                if i:
                    core_copy(h, own, g_fwd.at[h, j, i], sib, z).wait_send()


def local(basis_rows, energies, integrals, core_amps, denominators):
    n, m = lax.axis_size("pair"), lax.axis_size("cores")
    nc = n // 2
    S, R = basis_rows.shape
    A = integrals.shape[1]
    o = core_amps.shape[0]
    blk, K = o * m, o * n
    D = A + K
    H = 2
    w = R // H
    owner = lax.axis_index("pair") * m + lax.axis_index("cores")
    own_denoms = lax.dynamic_slice_in_dim(denominators, owner * o, o, 0)[:, None]
    dma = pltpu.SemaphoreType.DMA
    vmem = pl.BlockSpec(memory_space=pltpu.VMEM)
    anyspace = pl.BlockSpec(memory_space=pl.ANY)
    flops = 2 * S * R * (D + R)
    return pl.pallas_call(
        functools.partial(kernel, n, m, H),
        out_shape=(
            jax.ShapeDtypeStruct((o, R), F32),
            jax.ShapeDtypeStruct((S, R), BF16),
        ),
        in_specs=[anyspace, vmem, anyspace, anyspace, vmem, vmem],
        out_specs=(vmem, anyspace),
        scratch_shapes=[
            pltpu.VMEM((S, R), BF16),
            pltpu.VMEM((S, A), BF16),
            pltpu.VMEM((D, S), BF16),
            pltpu.VMEM((nc, D, blk), BF16),
            pltpu.VMEM((nc, D, blk), BF16),
            pltpu.VMEM((nc, D, blk), BF16),
            pltpu.VMEM((nc, D, blk), BF16),
            pltpu.VMEM((D, blk), BF16),
            pltpu.VMEM((blk, D), BF16),
            pltpu.VMEM((n, A, blk), BF16),
            pltpu.VMEM((K, R), BF16),
            pltpu.VMEM((H, blk, w), F32),
            pltpu.VMEM((H, blk, w), BF16),
            pltpu.VMEM((H, m, o, w), BF16),
            pltpu.VMEM((H, R, w), BF16),
            pltpu.VMEM((2, 512, w), BF16),
            dma((3,)), dma((2,)),
            dma((nc,)), dma((nc,)), dma((n,)),
            dma((nc,)), dma((nc,)), dma((nc,)), dma((nc,)),
            dma((nc,)), dma((nc,)), dma((n,)),
            dma((H, m)), dma((H, m)), dma((H, m)),
            dma((H, m, nc)), dma((H, m, nc)), dma((H, n * m)),
        ],
        compiler_params=pltpu.CompilerParams(
            collective_id=0, has_side_effects=True, vmem_limit_bytes=60 * 2**20
        ),
        cost_estimate=pl.CostEstimate(
            flops=flops, bytes_accessed=2 * S * (2 * R + A), transcendentals=0
        ),
    )(basis_rows, energies[None, :], integrals, core_amps, own_denoms, denominators[None, :])


def solution(mesh):
    in_specs = (P("pair", None), P("pair"), P("pair", "cores"), P(("pair", "cores"), None), P())
    out_specs = (P(("pair", "cores"), None), P("pair", None))
    return jax.shard_map(local, mesh=mesh, in_specs=in_specs, out_specs=out_specs, check_vma=False)
```

time: 393 us -> 197 us (0.50)
  waiting for transfers between devices: 287 us -> 0 us
  Pallas kernels: 0 us -> 182 us
  matrix products: 56.9 us -> 0 us
  local copies, waits for them, and re-layouts: 26.4 us -> 11.8 us
  between operations: 14.2 us -> 0.64 us
  other arithmetic: 4.18 us -> 0 us
    pallas_call x0 -> x1, Pallas kernels: none -> 182 us  [local(): pl.pallas_call(functools.partial(kernel, n, m, H), out_shape=(jax.ShapeDt...]
    reduce_scatter x3 -> x0, waiting for transfers between devices: 170 us -> none  [the longest x1 72.2 us: local(): lax.psum_scatter(partial_value, 'pair', scatter_dimension=0, tiled=True)]
    all_gather x3 -> x0, waiting for transfers between devices: 116 us -> none  [the longest x1 78.6 us: local(): lax.all_gather(core_b, ('pair', 'cores'), axis=0, tiled=True)]
    dot_general x5 -> x0, matrix products: 56.9 us -> none  [the longest x2 25.8 us: contract_rows(): lax.dot_general(left, right, (((0,), (0,)), ((), ())), preferred_element_...]
    unnamed x10 -> x2, local copies, waits for them, and re-layouts: 24.5 us -> 10.3 us
    convert_element_type x2 -> x0, other arithmetic: 4.18 us -> none  [the longest x1 2.09 us: local(): projected_b = projected.astype(jnp.bfloat16)]
  transfers between devices with their start and end apart: 6 -> 0, of which waited for: 6 -> 0; matrix products, arithmetic and copies ran while one was open for 7% -> 0% of each run, Pallas kernels for 0% -> 0%
where the time goes in v1:
time: 197 us; the launch traced here: 194 us
  Pallas kernels  182 us (92%)
  local copies, waits for them, and re-layouts  11.8 us (6%)
    pallas_call x1, Pallas kernels, local(): pl.pallas_call(functools.partial(kernel, n, m, H), out_shape=(jax.ShapeDt...  182 us
    unnamed x2, local copies, waits for them, and re-layouts  10.3 us

profile of v1, /device:TPU:26, one launch (start us, length us, event | category | flops | bytes accessed | tf_op | source)
XLA Modules:
  0.0 194.3 jit_solution(14378758836701325843)
XLA Ops:
  0.6 0.8 dynamic-slice_bitcast_fusion
  1.4 0.7 copy.7.own_denoms
  2.1 181.9 %shard_map.68 = (f32[64,2048]{1,0:T(8,128)}, bf16[2048,2048]{1,0:T(8,128)(2,1)}) custom-call(bf16[2048,2048]{1,0:T(8,128)(2,1)} %basis_hbm.1, f32[1,2048]{1,0:T(1,128)} %bitcast.4, bf16[2048,1024]{1,0:T(8,128)(2,1)} %integrals_hbm.1, bf16[64,2048]{1,0:T(8,128)(2,1)} %core_hbm.1, f32[64,1]{1,0:T(8,128)} %copy.7.own_denoms, f32[1,2048]{1,0:T(1,128)} %bitcast.5), custom_call_target="tpu_custom_call" | custom-call | flops 30064771072 | bytes 20971520 | tf_op jit(solution)/shard_map/pallas_call | solution.py:313
  184.0 1.9 copy.10
  185.8 8.4 %copy.11 = bf16[2048,2048]{1,0:T(8,128)(2,1)} copy(bf16[2048,2048]{1,0:T(8,128)(2,1)} %get-tuple-element.5) | data formatting | bytes 16777216

commit v2 on v1

v2 whole, which is shorter than its diff:
```python
import functools

import jax
import jax.numpy as jnp
from jax import lax
from jax.experimental import pallas as pl
from jax.experimental.pallas import tpu as pltpu
from jax.sharding import PartitionSpec as P

F32 = jnp.float32
BF16 = jnp.bfloat16
MESH = pl.DeviceIdType.MESH


def dot_nn(left, right):
    return lax.dot_general(left, right, (((1,), (0,)), ((), ())), preferred_element_type=F32)


def dot_nt(left, right):
    return lax.dot_general(left, right, (((1,), (1,)), ((), ())), preferred_element_type=F32)


def one_hot(rows, columns, column_of):
    row = lax.broadcasted_iota(jnp.int32, (rows, columns), 0)
    column = lax.broadcasted_iota(jnp.int32, (rows, columns), 1)
    return jnp.where(column == column_of(row), 1.0, 0.0).astype(BF16)


def kernel(
    n, m, H,
    basis_hbm, energies, integrals_hbm, core_hbm, own_denoms, denoms,
    next_ref, amps_hbm,
    basis, ints, left, sib_out, sib_in, summed, peer_in, relay_in, final, final_t, p_all, c_all,
    term, term_b, z_in, core_all, stage,
    load_sem, out_sem, c_send, c_fwd, c_rel, c_recv, c_recv_d,
    s_send, s_recv, x_send, x_recv, y_send, y_recv,
    p_send, p_fwd, p_rel, p_recv, p_recv_d, z_send, z_recv,
    zg_send, g_send, g_fwd, g_rel, g_recv, g_recv_d,
):
    me, z = lax.axis_index("pair"), lax.axis_index("cores")
    nc = n // 2
    chip, c = me // 2, lax.rem(me, 2)
    sib = chip * 2 + 1 - c
    S, R = basis.shape
    A = ints.shape[1]
    K, blk = R // m, R // n
    o = blk // m
    w = R // H
    D = A + K
    TM = D // 2
    relay = nc == 4 and o % 32 == 0

    def chip_at(i, step):
        if not relay:
            return lax.rem(chip + (i if step > 0 else nc - i), nc)
        high, low = chip // 2, lax.rem(chip, 2)
        high = 1 - high if i // 2 else high
        low = 1 - low if i % 2 else low
        return high * 2 + low

    def peer(i):
        return chip_at(i, 1) * 2 + c

    def back(i):
        return chip_at(i, -1) * 2 + c

    def other(i):
        return chip_at(i, -1) * 2 + 1 - c

    def rc(src, dst, ssem, rsem, pair, zz):
        return pltpu.make_async_remote_copy(
            src_ref=src, dst_ref=dst, send_sem=ssem, recv_sem=rsem,
            device_id=(pair, zz), device_id_type=MESH,
        )

    load_i = pltpu.make_async_copy(integrals_hbm, ints, load_sem.at[0])
    load_b = pltpu.make_async_copy(basis_hbm, basis, load_sem.at[1])

    def c_rows(s, k=None):
        if k is None:
            return c_all.at[pl.ds(pl.multiple_of(s * o, o), o), :]
        part = o // 2
        return c_all.at[pl.ds(pl.multiple_of(s * o + k * part, part), part), :]

    load_c = pltpu.make_async_copy(core_hbm, c_rows(me), load_sem.at[2])
    load_c.start()
    load_i.start()
    load_b.start()

    barrier = pltpu.get_barrier_semaphore()
    pl.semaphore_signal(barrier, inc=1, device_id=(sib, z), device_id_type=MESH)
    for i in range(1, nc):
        pl.semaphore_signal(barrier, inc=1, device_id=(peer(i), z), device_id_type=MESH)
    for j in range(1, m):
        pl.semaphore_signal(
            barrier, inc=1, device_id=(me, lax.rem(z + j, m)), device_id_type=MESH
        )
    pl.semaphore_wait(barrier, nc + m - 1)

    def gather(slot, send, fwd, rel, recv, recv_d):
        near = [1, 2] if relay else list(range(1, nc))

        def start():
            for i in near + [0]:
                to = peer(i) if i else sib
                rc(slot(me), slot(me), send(i), recv(me), to, z).start()

        def half(s, k, to):
            return rc(slot(s, k), slot(s, k), rel(k), recv_d() if k else recv(s), to, z)

        def forward():
            for i in near:
                s = back(i)
                copy = rc(slot(s), slot(s), fwd(i), recv(s), sib, z)
                copy.wait_recv()
                if relay:
                    half(s, i - 1, peer(3 - i)).start()
                copy.start()

        def tail():
            if relay:
                s = back(3)
                half(s, 0, sib).wait_recv()
                half(s, 1, sib).wait_recv()
                rc(slot(s), slot(s), fwd(3), recv(s), sib, z).start()

        def other_arrived(i):
            s = other(i)
            rc(slot(s), slot(s), send(0), recv(s), sib, z).wait_recv()

        def sent():
            for i in near + [0]:
                rc(slot(me), slot(me), send(i), recv(me), sib, z).wait_send()
            for i in range(1, nc):
                rc(slot(me), slot(me), fwd(i), recv(me), sib, z).wait_send()
            if relay:
                half(me, 0, sib).wait_send()
                half(me, 1, sib).wait_send()

        return start, forward, tail, other_arrived, sent

    load_c.wait()
    c_start, c_forward, c_tail, c_other, c_sent = gather(
        c_rows, lambda i: c_send.at[i], lambda i: c_fwd.at[i], lambda k: c_rel.at[k],
        lambda s: c_recv.at[s], lambda: c_recv_d.at[0],
    )
    c_start()

    load_i.wait()
    TA = 256
    eye = one_hot(TA, TA, lambda row: row)

    @pl.loop(0, A // TA)
    def _(t):
        at = pl.multiple_of(t * TA, TA)
        left[pl.ds(at, TA), :] = dot_nt(eye, ints[:, pl.ds(at, TA)]).astype(BF16)

    load_b.wait()
    TK = 128
    pick = one_hot(TK, TK * m, lambda row: (row // o) * blk + z * o + lax.rem(row, o))

    @pl.loop(0, K // TK)
    def _(t):
        kept = dot_nt(pick, basis[:, pl.ds(pl.multiple_of(t * TK * m, TK * m), TK * m)])
        left[pl.ds(pl.multiple_of(A + t * TK, TK), TK), :] = (kept * energies[...]).astype(BF16)

    def sib_copy(i):
        return rc(sib_out.at[i], sib_in.at[i], s_send.at[i], s_recv.at[i], sib, z)

    def peer_copy(i):
        return rc(summed.at[i], peer_in.at[i], x_send.at[i], x_recv.at[i], peer(i), z)

    def partial_block(pair, dst):
        col = pl.ds(pl.multiple_of(pair * blk, blk), blk)

        @pl.loop(0, 2)
        def _(t):
            rows = pl.ds(pl.multiple_of(t * TM, TM), TM)
            dst[rows, :] = dot_nn(left[rows, :], basis[:, col]).astype(BF16)

    hd = D // 2

    def relay_copy(k):
        return rc(
            summed.at[3, pl.ds(k * hd, hd), :], relay_in.at[k],
            y_send.at[k], y_recv.at[k], peer(k + 1), z,
        )

    def combine(i):
        sib_copy(i).wait_recv()
        passed = None
        if relay and i < 3:
            passed = 2 - i
            relay_copy(passed).wait_recv()

        for k in range(2):
            @pl.loop(0, hd // 128)
            def _(t):
                at = pl.ds(pl.multiple_of(t * 128, 128), 128)
                rows = pl.ds(pl.multiple_of(k * hd + t * 128, 128), 128)
                value = summed[i, rows, :].astype(F32) + sib_in[i, rows, :].astype(F32)
                if passed == k:
                    value += relay_in[k, at, :].astype(F32)
                summed[i, rows, :] = value.astype(BF16)

        if relay and i == 3:
            relay_copy(0).start()
            relay_copy(1).start()
        else:
            peer_copy(i).start()

    def sib_part(i):
        partial_block(peer(i) + 1 - 2 * c, sib_out.at[i])
        sib_copy(i).start()

    def own_part(i):
        partial_block(peer(i), summed.at[i])

    if relay:
        sib_part(3)
        own_part(3)
        sib_part(1)
        combine(3)
        own_part(1)
        c_forward()
        sib_part(2)
        own_part(2)
        combine(1)
        sib_part(0)
        combine(2)
        own_part(0)
        c_tail()
    else:
        order = list(range(nc - 1, 0, -1)) + [0]
        for k, i in enumerate(order):
            sib_part(i)
            if k >= 1:
                combine(order[k - 1])
            own_part(i)
        c_forward()

    sib_copy(0).wait_recv()
    direct = [1, 2] if relay else list(range(1, nc))
    for i in direct:
        peer_copy(i).wait_recv()

    @pl.loop(0, D // 128)
    def _(t):
        rows = pl.ds(pl.multiple_of(t * 128, 128), 128)
        total = summed[0, rows, :].astype(F32) + sib_in[0, rows, :].astype(F32)
        for i in direct:
            total += peer_in[i, rows, :].astype(F32)
        final[rows, :] = total.astype(BF16)

    def p_slot(s, k=None):
        return p_all.at[s] if k is None else p_all.at[s, pl.ds(k * (A // 2), A // 2), :]

    p_all[me] = final[0:A, :]
    p_start, p_forward, p_tail, p_other, p_sent = gather(
        p_slot, lambda i: p_send.at[i], lambda i: p_fwd.at[i], lambda k: p_rel.at[k],
        lambda s: p_recv.at[s], lambda: p_recv_d.at[0],
    )
    p_start()
    final_t[...] = dot_nt(one_hot(blk, blk, lambda row: row), final[...]).astype(BF16)
    for i in range(nc):
        c_other(i)

    def z_copy(q, j):
        rows = pl.ds(pl.multiple_of(lax.rem(z + j, m) * o, o), o)
        return rc(
            term_b.at[q, rows, :], z_in.at[q, j], z_send.at[q, j], z_recv.at[q, j],
            me, lax.rem(z + j, m),
        )

    def add_term(q):
        value = dot_nn(final_t[:, 0:A], p_all[q])
        value += dot_nn(final_t[:, A:D], c_all[:, pl.ds(pl.multiple_of(q * blk, blk), blk)])
        term[q] = value
        term_b[q] = value.astype(BF16)
        for j in range(1, m):
            z_copy(q, j).start()

    add_term(me)
    p_other(0)
    add_term(sib)
    p_forward()
    for i in direct:
        add_term(back(i))
    for i in direct:
        p_other(i)
        add_term(other(i))
    p_tail()
    if relay:
        add_term(back(3))
        p_other(3)
        add_term(other(3))

    own = me * m + z

    def core_gather(h, j):
        zz = lax.rem(z + m - j, m)

        def slot(s, k=None):
            at = (s * m + zz) * o
            if k is None:
                return core_all.at[h, pl.ds(pl.multiple_of(at, o), o), :]
            part = o // 2
            return core_all.at[h, pl.ds(pl.multiple_of(at + k * part, part), part), :]

        return gather(
            slot, lambda i: g_send.at[h, j, i], lambda i: g_fwd.at[h, j, i],
            lambda k: g_rel.at[h, j, k], lambda s: g_recv.at[h, s * m + zz],
            lambda: g_recv_d.at[h, j],
        )

    def along_z(h, j, owner):
        rows = core_all.at[h, pl.ds(pl.multiple_of(owner * o, o), o), :]
        return rc(rows, rows, zg_send.at[h, j], g_recv.at[h, owner], me, lax.rem(z + j, m))

    per = n // H
    for h in range(H):
        for k in range(per):
            q = h * per + k
            for j in range(1, m):
                z_copy(q, j).wait_recv()
            cols = pl.ds(q * blk, blk)
            total = term[q, pl.ds(pl.multiple_of(z * o, o), o), :]
            for j in range(1, m):
                total += z_in[q, j].astype(F32)
            current = c_all[pl.ds(pl.multiple_of(me * o, o), o), cols].astype(F32)
            value = current - total / (own_denoms[...] + denoms[:, cols])
            next_ref[:, cols] = value
            core_all[h, pl.ds(pl.multiple_of(own * o, o), o), k * blk:(k + 1) * blk] = (
                value.astype(BF16)
            )
        for j in range(1, m):
            along_z(h, j, own).start()
        core_gather(h, 0)[0]()

    def each_z(step, h, first=0):
        @pl.loop(first, m)
        def _(j):
            core_gather(h, j)[step]()

    def from_z(h):
        @pl.loop(1, m)
        def _(j):
            along_z(h, 1, me * m + lax.rem(z + m - j, m)).wait_recv()
            core_gather(h, j)[0]()

    TR, TN = 1024, 256
    writes = []

    def rows_of(h):
        @pl.loop(0, m)
        def _(j):
            for i in range(nc):
                core_gather(h, j)[3](i)

        for t in range(S // TR):
            b = len(writes) % 2
            if len(writes) >= 2:
                writes[-2].wait()

            @pl.loop(0, w // TN)
            def _(k):
                col = pl.ds(pl.multiple_of(k * TN, TN), TN)
                stage[b, :, col] = dot_nn(
                    basis[t * TR:(t + 1) * TR, :], core_all[h, :, col]
                ).astype(BF16)

            copy = pltpu.make_async_copy(
                stage.at[b], amps_hbm.at[pl.ds(t * TR, TR), pl.ds(h * w, w)], out_sem.at[b]
            )
            copy.start()
            writes.append(copy)

    for step in range(H + 3):
        if step < H:
            from_z(step)
        if 0 <= step - 1 < H:
            each_z(1, step - 1)
        if 0 <= step - 2 < H:
            each_z(2, step - 2)
        if 0 <= step - 3 < H:
            rows_of(step - 3)
    for copy in writes[-2:]:
        copy.wait()

    c_sent()
    p_sent()
    for i in range(nc):
        sib_copy(i).wait_send()
    for i in direct:
        peer_copy(i).wait_send()
    if relay:
        relay_copy(0).wait_send()
        relay_copy(1).wait_send()

    @pl.loop(0, n)
    def _(q):
        for j in range(1, m):
            z_copy(q, j).wait_send()

    for h in range(H):
        for j in range(1, m):
            along_z(h, j, own).wait_send()
        each_z(4, h)


def local(basis_rows, energies, integrals, core_amps, denominators):
    n, m = lax.axis_size("pair"), lax.axis_size("cores")
    nc = n // 2
    S, R = basis_rows.shape
    A = integrals.shape[1]
    o = core_amps.shape[0]
    blk, K = o * m, o * n
    D = A + K
    H = 4
    w = R // H
    owner = lax.axis_index("pair") * m + lax.axis_index("cores")
    own_denoms = lax.dynamic_slice_in_dim(denominators, owner * o, o, 0)[:, None]
    dma = pltpu.SemaphoreType.DMA
    vmem = pl.BlockSpec(memory_space=pltpu.VMEM)
    anyspace = pl.BlockSpec(memory_space=pl.ANY)
    flops = 2 * S * R * (D + R)
    return pl.pallas_call(
        functools.partial(kernel, n, m, H),
        out_shape=(
            jax.ShapeDtypeStruct((o, R), F32),
            jax.ShapeDtypeStruct((S, R), BF16),
        ),
        in_specs=[anyspace, vmem, anyspace, anyspace, vmem, vmem],
        out_specs=(vmem, anyspace),
        scratch_shapes=[
            pltpu.VMEM((S, R), BF16),
            pltpu.VMEM((S, A), BF16),
            pltpu.VMEM((D, S), BF16),
            pltpu.VMEM((nc, D, blk), BF16),
            pltpu.VMEM((nc, D, blk), BF16),
            pltpu.VMEM((nc, D, blk), BF16),
            pltpu.VMEM((nc, D, blk), BF16),
            pltpu.VMEM((2, D // 2, blk), BF16),
            pltpu.VMEM((D, blk), BF16),
            pltpu.VMEM((blk, D), BF16),
            pltpu.VMEM((n, A, blk), BF16),
            pltpu.VMEM((K, R), BF16),
            pltpu.VMEM((n, blk, blk), F32),
            pltpu.VMEM((n, blk, blk), BF16),
            pltpu.VMEM((n, m, o, blk), BF16),
            pltpu.VMEM((H, R, w), BF16),
            pltpu.VMEM((2, 1024, w), BF16),
            dma((3,)), dma((2,)),
            dma((nc,)), dma((nc,)), dma((2,)), dma((n,)), dma((1,)),
            dma((nc,)), dma((nc,)), dma((nc,)), dma((nc,)), dma((2,)), dma((2,)),
            dma((nc,)), dma((nc,)), dma((2,)), dma((n,)), dma((1,)), dma((n, m)), dma((n, m)),
            dma((H, m)), dma((H, m, nc)), dma((H, m, nc)), dma((H, m, 2)),
            dma((H, n * m)), dma((H, m)),
        ],
        compiler_params=pltpu.CompilerParams(
            collective_id=0, has_side_effects=True, vmem_limit_bytes=60 * 2**20
        ),
        cost_estimate=pl.CostEstimate(
            flops=flops, bytes_accessed=2 * S * (2 * R + A), transcendentals=0
        ),
    )(basis_rows, energies[None, :], integrals, core_amps, own_denoms, denominators[None, :])


def solution(mesh):
    in_specs = (P("pair", None), P("pair"), P("pair", "cores"), P(("pair", "cores"), None), P())
    out_specs = (P(("pair", "cores"), None), P("pair", None))
    return jax.shard_map(local, mesh=mesh, in_specs=in_specs, out_specs=out_specs, check_vma=False)
```

time: 197 us -> 152 us (0.77); the launches traced: 194 us -> 151 us
  Pallas kernels: 182 us -> 139 us
    pallas_call x1, Pallas kernels: 182 us -> 139 us  [local(): pl.pallas_call(functools.partial(kernel, n, m, H), out_shape=(jax.ShapeDt...]
where the time goes in v2:
time: 152 us; the launch traced here: 151 us
  Pallas kernels  139 us (91%)
  local copies, waits for them, and re-layouts  11.8 us (8%)
    pallas_call x1, Pallas kernels, local(): pl.pallas_call(functools.partial(kernel, n, m, H), out_shape=(jax.ShapeDt...  139 us
    unnamed x2, local copies, waits for them, and re-layouts  10.3 us

profile of v2, /device:TPU:26, one launch (start us, length us, event | category | flops | bytes accessed | tf_op | source)
XLA Modules:
  0.0 151.3 jit_solution(36777860113027683)
XLA Ops:
  0.6 0.8 dynamic-slice_bitcast_fusion
  1.4 0.7 copy.7.own_denoms
  2.1 138.8 %shard_map.68 = (f32[64,2048]{1,0:T(8,128)}, bf16[2048,2048]{1,0:T(8,128)(2,1)}) custom-call(bf16[2048,2048]{1,0:T(8,128)(2,1)} %basis_hbm.1, f32[1,2048]{1,0:T(1,128)} %bitcast.4, bf16[2048,1024]{1,0:T(8,128)(2,1)} %integrals_hbm.1, bf16[64,2048]{1,0:T(8,128)(2,1)} %core_hbm.1, f32[64,1]{1,0:T(8,128)} %copy.7.own_denoms, f32[1,2048]{1,0:T(1,128)} %bitcast.5), custom_call_target="tpu_custom_call" | custom-call | flops 30064771072 | bytes 20971520 | tf_op jit(solution)/shard_map/pallas_call | solution.py:427
  140.9 1.9 %copy.10 = f32[64,2048]{1,0:T(8,128)} copy(f32[64,2048]{1,0:T(8,128)} %get-tuple-element.4) | data formatting | bytes 1048576
  142.8 8.4 %copy.11 = bf16[2048,2048]{1,0:T(8,128)(2,1)} copy(bf16[2048,2048]{1,0:T(8,128)(2,1)} %get-tuple-element.5) | data formatting | bytes 16777216

commit v3 on v2

--- a/solution.py
+++ b/solution.py
@@ -416,7 +416,7 @@
     o = core_amps.shape[0]
     blk, K = o * m, o * n
     D = A + K
-    H = 4
+    H = 2
     w = R // H
     owner = lax.axis_index("pair") * m + lax.axis_index("cores")
     own_denoms = lax.dynamic_slice_in_dim(denominators, owner * o, o, 0)[:, None]

time: 152 us -> 159 us (1.046)
  Pallas kernels: 139 us -> 146 us
    pallas_call x1, Pallas kernels: 139 us -> 146 us  [local(): pl.pallas_call(functools.partial(kernel, n, m, H), out_shape=(jax.ShapeDt...]
where the time goes in v3:
time: 159 us; the launch traced here: 158 us
  Pallas kernels  146 us (92%)
  local copies, waits for them, and re-layouts  11.8 us (7%)
    pallas_call x1, Pallas kernels, local(): pl.pallas_call(functools.partial(kernel, n, m, H), out_shape=(jax.ShapeDt...  146 us
    unnamed x2, local copies, waits for them, and re-layouts  10.3 us

profile of v3, /device:TPU:26, one launch (start us, length us, event | category | flops | bytes accessed | tf_op | source)
XLA Modules:
  0.0 158.4 jit_solution(12520716362609950367)
XLA Ops:
  0.6 0.8 dynamic-slice_bitcast_fusion
  1.4 0.7 copy.7.own_denoms
  2.1 146.0 %shard_map.68 = (f32[64,2048]{1,0:T(8,128)}, bf16[2048,2048]{1,0:T(8,128)(2,1)}) custom-call(bf16[2048,2048]{1,0:T(8,128)(2,1)} %basis_hbm.1, f32[1,2048]{1,0:T(1,128)} %bitcast.4, bf16[2048,1024]{1,0:T(8,128)(2,1)} %integrals_hbm.1, bf16[64,2048]{1,0:T(8,128)(2,1)} %core_hbm.1, f32[64,1]{1,0:T(8,128)} %copy.7.own_denoms, f32[1,2048]{1,0:T(1,128)} %bitcast.5), custom_call_target="tpu_custom_call" | custom-call | flops 30064771072 | bytes 20971520 | tf_op jit(solution)/shard_map/pallas_call | solution.py:427
  148.1 1.9 %copy.10 = f32[64,2048]{1,0:T(8,128)} copy(f32[64,2048]{1,0:T(8,128)} %get-tuple-element.4) | data formatting | bytes 1048576
  150.0 8.4 %copy.11 = bf16[2048,2048]{1,0:T(8,128)(2,1)} copy(bf16[2048,2048]{1,0:T(8,128)(2,1)} %get-tuple-element.5) | data formatting | bytes 16777216
